TPU v7x, 32 devices: a whole 2x2x4 slice. The times are simulated.
32 devices in a mesh: dp: 8 (over y, x, core), tensor: 4 (over z).
Axes of the slice: x: 2, y: 2, z: 4, core: 2. Of those that a mesh axis runs over, the one named last changes fastest.
Arguments:
- out_grad: bfloat16 [8, 256, 4096], P('dp', 'tensor'), may hold values from -6 to 6
- out_weight: bfloat16 [4096, 1024], P('dp', 'tensor'), may hold values from -0.1875 to 0.1875
- queries: bfloat16 [8, 256, 1024], P('dp', None, 'tensor'), may hold values from -5 to 5
- keys: bfloat16 [8, 256, 512], P('dp', None, 'tensor'), may hold values from -5 to 5, as said below
- values: bfloat16 [8, 256, 512], P('dp', None, 'tensor'), may hold values from -6 to 6, as said below
- segment_ids: int32 [8, 256], P('dp'), may hold values from 0 to 3, never falling along the last dimension, each value on 1 to 128 neighbouring positions
Outputs:
- d_queries: bfloat16 [8, 256, 1024], P('dp', None, 'tensor')
- d_keys: bfloat16 [8, 256, 512], P('dp', None, 'tensor')
- d_values: bfloat16 [8, 256, 512], P('dp', None, 'tensor')
- d_out_weight: float32 [4096, 1024], P('dp', 'tensor')
Inputs may be any that keep to these rules, and one draw needn't show every extreme that they name: `keys`: column blocks 2 g and 2 g + 1 are equal. `values`: column blocks 2 g and 2 g + 1 are equal.
All inputs are finite; a program needn't handle non-finite values.
Results may differ from a plain program's by a relative error of at most 0.018.
Values may be sent and summed in bfloat16 or wider, within the bound.
A program may use at most 128 MiB of HBM per device.

v0:
```python
import jax
import jax.numpy as jnp
from jax import lax
from jax.sharding import PartitionSpec as P

HD = 128


def from_partner(block, axis, bit):
    count = lax.axis_size(axis)
    route = []
    for low in range(count):
        high = low | 1 << bit
        if high != low and high < count:
            route += [(low, high), (high, low)]
    return lax.ppermute(block, axis, route)


def local(out_grad, out_weight, queries, keys, values, segment_ids):
    scale = HD ** (-0.5)
    grad_local = out_grad[0]
    query_rows = queries[0]
    length = query_rows.shape[0]
    width = query_rows.shape[1]
    heads_here = width // HD
    key_local = keys[0]
    value_local = values[0]
    query_heads = query_rows.reshape(length, heads_here, HD)
    scores = (
        jnp.einsum("qhd,kd->hqk", query_heads, key_local, preferred_element_type=jnp.float32)
        * scale
    )
    segments = segment_ids[0]
    position = jnp.arange(length)
    visible = (segments[:, None] == segments[None, :]) & (position[:, None] >= position[None, :])
    masked = jnp.where(visible[None], scores, -jnp.inf)
    top_score = jnp.max(masked, axis=-1, keepdims=True)
    raw_exp = jnp.exp(masked - top_score)
    attn_prob = raw_exp / jnp.sum(raw_exp, axis=-1, keepdims=True)
    prob_low = attn_prob.astype(jnp.bfloat16)
    attn_out = jnp.einsum(
        "hqk,kd->qhd", prob_low, value_local, preferred_element_type=jnp.float32
    ).astype(jnp.bfloat16)
    flat_out = attn_out.reshape(length, width)
    grad_full = lax.all_gather(grad_local, "tensor", axis=0, tiled=True)
    columns = grad_full
    grad_sum = jnp.dot(
        columns,
        lax.all_gather(out_weight, "dp", axis=0, tiled=True),
        preferred_element_type=jnp.float32,
    )
    columns = grad_full
    weight_rows = lax.psum_scatter(
        lax.dot_general(
            columns, flat_out, (((0,), (0,)), ((), ())), preferred_element_type=jnp.float32
        ).astype(jnp.bfloat16),
        "dp",
        scatter_dimension=0,
        tiled=True,
    ).astype(jnp.float32)
    grad_attn = grad_sum.astype(jnp.bfloat16)
    grad_heads = grad_attn.reshape(length, heads_here, HD)
    deltas = jnp.sum(grad_heads.astype(jnp.float32) * attn_out.astype(jnp.float32), axis=-1)
    grad_values = jnp.einsum(
        "hqk,qhd->kd", prob_low, grad_heads, preferred_element_type=jnp.float32
    )
    grad_prob = jnp.einsum(
        "qhd,kd->hqk", grad_heads, value_local, preferred_element_type=jnp.float32
    )
    grad_score = (attn_prob * (grad_prob - jnp.transpose(deltas)[:, :, None]) * scale).astype(
        jnp.bfloat16
    )
    grad_queries = jnp.einsum(
        "hqk,kd->qhd", grad_score, key_local, preferred_element_type=jnp.float32
    ).astype(jnp.bfloat16)
    grad_keys = jnp.einsum(
        "hqk,qhd->kd", grad_score, query_heads, preferred_element_type=jnp.float32
    )
    partner_keys, partner_values = (
        from_partner(grad_keys.astype(jnp.bfloat16), "tensor", 0).astype(grad_keys.dtype),
        from_partner(grad_values.astype(jnp.bfloat16), "tensor", 0).astype(grad_values.dtype),
    )
    keys_total = (grad_keys + partner_keys).astype(jnp.bfloat16)
    values_total = (grad_values + partner_values).astype(jnp.bfloat16)
    weight_grad = weight_rows / lax.axis_size("dp")
    return (
        grad_queries.reshape(1, length, width),
        keys_total[None],
        values_total[None],
        weight_grad,
    )


def solution(mesh):
    in_specs = (
        P("dp", "tensor", None),
        P("dp", "tensor"),
        P("dp", None, "tensor"),
        P("dp", None, "tensor"),
        P("dp", None, "tensor"),
        P("dp", None),
    )
    out_specs = (
        P("dp", None, "tensor"),
        P("dp", None, "tensor"),
        P("dp", None, "tensor"),
        P("dp", "tensor"),
    )
    return jax.shard_map(local, mesh=mesh, in_specs=in_specs, out_specs=out_specs, check_vma=False)
```

profile of v0, /device:TPU:0, one launch (start us, length us, event | category | flops | bytes accessed | tf_op | source)
XLA Modules:
  0.0 143.6 jit_solution(18421356278678418032)
XLA Ops:
  7.2 0.0 copy-start
  7.2 0.0 all-gather.6.cloned.1.call-start
  7.2 0.7 all-gather.6.cloned.1.call-update
  7.9 0.0 all-gather.4.cloned.1.call-start
  8.0 0.7 all-gather.4.cloned.1.call-update
  8.7 0.0 reduce-scatter.2.cloned.1.call-start
  8.7 0.9 reshape_squeeze.3
  9.7 0.9 fusion.16
  10.5 0.0 copy-done
  10.5 0.3 fusion.55
  10.9 47.4 %all-gather.6.cloned.1.call-done = bf16[1,256,4096]{2,1,0:T(8,128)(2,1)} async-done(((bf16[1,64,4096]{2,1,0:T(8,128)(2,1)}), bf16[1,256,4096]{2,1,0:T(8,128)(2,1)}) %all-gather.6.cloned.1.call-update) | async-done | bytes 2097168 | tf_op jit(solution)/shard_map/all_gather | solution.py:45
  58.3 28.5 %all-gather.4.cloned.1.call-done = bf16[4096,256]{1,0:T(8,128)(2,1)} async-done(((bf16[512,256]{1,0:T(8,128)(2,1)}), bf16[4096,256]{1,0:T(8,128)(2,1)}) %all-gather.4.cloned.1.call-update) | async-done | bytes 2097168 | tf_op jit(solution)/shard_map/all_gather | solution.py:49
  86.8 3.1 %fusion.13 = bf16[256,256]{0,1:T(8,128)(2,1)S(1)} fusion(bf16[4096,256]{1,0:T(8,128)(2,1)} %all-gather.4.cloned.1.call-done, bf16[1,256,4096]{2,1,0:T(8,128)(2,1)} %all-gather.6.cloned.1.call-done), kind=kOutput, calls=%fused_computation.18 | convolution fusion | flops 536936448 | bytes 4325376 | tf_op jit(solution)/shard_map/dot_general | solution.py:47
  89.9 0.0 copy-start.1
  90.0 0.5 multiply_reduce_fusion
  90.5 1.0 copy-done.1
  91.5 2.1 %fusion.1 = bf16[4096,256]{0,1:T(8,128)(2,1)} fusion(bf16[256,256]{0,1:T(8,128)(2,1)S(1)} %bitcast.105, bf16[1,256,4096]{2,1,0:T(8,128)(2,1)S(1)} %copy-done.1), kind=kOutput, calls=%fused_computation.2 | convolution fusion | flops 537919488 | bytes 4325376 | tf_op jit(solution)/shard_map/dot_general | solution.py:54
  93.6 0.0 reduce-scatter.2.cloned.1.call-update
  93.6 0.2 fusion.12
  93.8 0.2 fusion.64
  94.1 1.5 %collective-permute-start = (bf16[256,128]{1,0:T(8,128)(2,1)S(1)}, bf16[256,128]{1,0:T(8,128)(2,1)S(1)}, u32[]{:S(2)}, u32[]{:S(2)}) collective-permute-start(bf16[256,128]{1,0:T(8,128)(2,1)S(1)} %get-tuple-element.12), channel_id=1, source_target_pairs={{0,1},{1,0},{2,3},{3,2},{4,5},{5,4},{6,7},{7,6},{8,9},{9,8},{10,11... | collective-permute-start | bytes 196616 | tf_op jit(solution)/shard_map/ppermute | solution.py:16
  95.6 0.2 convolution_convert_fusion.1
  95.8 0.5 fusion.65
  96.4 0.8 copy.19
  97.1 0.5 collective-permute-start.1
  97.7 0.7 collective-permute-done
  98.4 0.6 fusion.20
  99.0 2.3 %collective-permute-done.1 = bf16[256,128]{1,0:T(8,128)(2,1)S(1)} collective-permute-done((bf16[256,128]{1,0:T(8,128)(2,1)S(1)}, bf16[256,128]{1,0:T(8,128)(2,1)S(1)}, u32[]{:S(2)}, u32[]{:S(2)}) %collective-permute-start.1) | collective-permute-done | bytes 65568 | tf_op jit(solution)/shard_map/ppermute | solution.py:16
  101.4 0.6 fusion.21
  102.0 33.0 %reduce-scatter.2.cloned.1.call-done = bf16[512,256]{0,1:T(8,128)(2,1)} async-done(((bf16[4096,256]{0,1:T(8,128)(2,1)}), bf16[512,256]{0,1:T(8,128)(2,1)}) %reduce-scatter.2.cloned.1.call-update) | async-done | bytes 262160 | tf_op jit(solution)/shard_map/reduce_scatter | solution.py:53
  135.0 1.0 convert_multiply_fusion
  136.0 1.0 copy.20
  (2 shorter events, 0.0 us)
Async XLA Ops:
  7.2 3.4 %copy-start = (bf16[1,256,128]{2,1,0:T(8,128)(2,1)S(1)}, bf16[1,256,128]{2,1,0:T(8,128)(2,1)}, u32[]{:S(2)}) copy-start(bf16[1,256,128]{2,1,0:T(8,128)(2,1)} %param.9) | copy-start | bytes 196612
  7.2 51.1 %all-gather.6.cloned.1.call-start = ((), (), s32[]{:S(2)}) async-start(), calls=%async_computation.3 | async-start | bytes 2621440 | tf_op jit(solution)/shard_map/all_gather | solution.py:45
  7.9 78.9 %all-gather.4.cloned.1.call-start = ((), (), s32[]{:S(2)}) async-start(), calls=%async_computation.1 | async-start | bytes 2359296 | tf_op jit(solution)/shard_map/all_gather | solution.py:49
  8.7 126.3 %reduce-scatter.2.cloned.1.call-start = ((), (), s32[]{:S(2)}) async-start(), calls=%async_computation.2 | async-start | bytes 2359296 | tf_op jit(solution)/shard_map/reduce_scatter | solution.py:53
  10.9 79.1 %copy-start.2 = (bf16[1,256,128]{2,1,0:T(8,128)(2,1)S(1)}, bf16[1,256,128]{2,1,0:T(8,128)(2,1)}, u32[]{:S(2)}) copy-start(bf16[1,256,128]{2,1,0:T(8,128)(2,1)} %param.10) | copy-start | bytes 196612
  89.9 1.6 %copy-start.1 = (bf16[1,256,4096]{2,1,0:T(8,128)(2,1)S(1)}, bf16[1,256,4096]{2,1,0:T(8,128)(2,1)}, u32[]{:S(2)}) copy-start(bf16[1,256,4096]{2,1,0:T(8,128)(2,1)} %all-gather.6.cloned.1.call-done) | copy-start | bytes 6291460
  94.1 4.3 %collective-permute-start = (bf16[256,128]{1,0:T(8,128)(2,1)S(1)}, bf16[256,128]{1,0:T(8,128)(2,1)S(1)}, u32[]{:S(2)}, u32[]{:S(2)}) collective-permute-start(bf16[256,128]{1,0:T(8,128)(2,1)S(1)} %get-tuple-element.12), channel_id=1, source_target_pairs={{0,1},{1,0},{2,3},{3,2},{4,5},{5,4},{6,7},{7,6},{8,9},{9,8},{10,11... | collective-permute-start | bytes 196616 | tf_op jit(solution)/shard_map/ppermute | solution.py:16
  97.1 4.3 %collective-permute-start.1 = (bf16[256,128]{1,0:T(8,128)(2,1)S(1)}, bf16[256,128]{1,0:T(8,128)(2,1)S(1)}, u32[]{:S(2)}, u32[]{:S(2)}) collective-permute-start(bf16[256,128]{1,0:T(8,128)(2,1)S(1)} %get-tuple-element.14), channel_id=1, source_target_pairs={{0,1},{1,0},{2,3},{3,2},{4,5},{5,4},{6,7},{7,6},{8,9},{9,8},{10,11... | collective-permute-start | bytes 196616 | tf_op jit(solution)/shard_map/ppermute | solution.py:16
Sparse Core Ops, SparseCore 0:
  9.6 48.6 all-gather.5
  60.1 26.5 all-gather.3
  93.7 41.2 reduce-scatter.1
where the time goes:
time: 144 us
  waiting for transfers between devices  113 us (78%)
  between operations  13.8 us (10%)
  matrix products  7.24 us (5%)
  local copies, waits for them, and re-layouts  3.77 us (3%)
  other arithmetic  3.15 us (2%)
  starting transfers between devices  2.2 us (2%)
    all_gather x1, waiting for transfers between devices, local(): grad_full = lax.all_gather(grad_local, 'tensor', axis=0, tiled=True)  47.4 us
    reduce_scatter x1, waiting for transfers between devices, local(): lax.psum_scatter(lax.dot_general(columns, flat_out, (((0,), (0,)), ((), (...  33 us
    all_gather x1, waiting for transfers between devices, local(): lax.all_gather(out_weight, 'dp', axis=0, tiled=True)  28.5 us
    dot_general x1, matrix products, local(): jnp.dot(columns, lax.all_gather(out_weight, 'dp', axis=0, tiled=True), pr...  3.15 us
    ppermute x2, waiting for transfers between devices, from_partner(): return lax.ppermute(block, axis, route)  3.08 us
  transfers between devices with their start and end apart: 5, of which 5 were waited for; matrix products, arithmetic and copies ran while one was open for 4% of the time, Pallas kernels for 0%

commit v1 on v0

--- a/solution.py
+++ b/solution.py
@@ -4,6 +4,28 @@
 from jax.sharding import PartitionSpec as P
 
 HD = 128
+
+
+def in_order(blocks, dim):
+    dims = list(blocks.shape[1:])
+    dims[dim] *= blocks.shape[0]
+    return jnp.moveaxis(blocks, 0, dim).reshape(dims)
+
+
+def gather_around(x, axis, dim):
+    length = lax.axis_size(axis)
+    pairs = [(i, (i + 1) % length) for i in range(length)]
+    back = [(b, a) for a, b in pairs]
+    lower, upper = ([], [])
+    for turn in range(length - 1):
+        if turn % 2 == 0:
+            lower.append(lax.ppermute(lower[-1] if lower else x, axis, pairs))
+        else:
+            upper.append(lax.ppermute(upper[-1] if upper else x, axis, back))
+    parts = jnp.stack([*lower[::-1], x, *upper])
+    shift = lax.axis_index(axis) - len(lower)
+    parts = parts[(jnp.arange(length) - shift) % length]
+    return in_order(parts, dim)
 
 
 def from_partner(block, axis, bit):
@@ -45,9 +67,7 @@
     grad_full = lax.all_gather(grad_local, "tensor", axis=0, tiled=True)
     columns = grad_full
     grad_sum = jnp.dot(
-        columns,
-        lax.all_gather(out_weight, "dp", axis=0, tiled=True),
-        preferred_element_type=jnp.float32,
+        columns, gather_around(out_weight, "dp", 0), preferred_element_type=jnp.float32
     )
     columns = grad_full
     weight_rows = lax.psum_scatter(

time: 144 us -> 114 us (0.79)
  waiting for transfers between devices: 113 us -> 68.2 us
  starting transfers between devices: 2.2 us -> 10.6 us
  local copies, waits for them, and re-layouts: 3.77 us -> 9.88 us
    all_gather x1, waiting for transfers between devices: 47.4 us -> 13.8 us  [local(): grad_full = lax.all_gather(grad_local, 'tensor', axis=0, tiled=True)]
    all_gather x1 -> x0, waiting for transfers between devices: 28.5 us -> none  [local(): lax.all_gather(out_weight, 'dp', axis=0, tiled=True)]
    ppermute x0 -> x7, waiting for transfers between devices: none -> 20 us  [the longest x4 20 us: gather_around(): lower.append(lax.ppermute(lower[-1] if lower else x, axis, pairs))]
    ppermute x0 -> x7, starting transfers between devices: none -> 8.38 us  [the longest x3 7.87 us: gather_around(): upper.append(lax.ppermute(upper[-1] if upper else x, axis, back))]
    unnamed x8 -> x21, local copies, waits for them, and re-layouts: 2.83 us -> 6.83 us
    gather x0 -> x1, local copies, waits for them, and re-layouts: none -> 1.99 us  [gather_around(): parts = parts[(jnp.arange(length) - shift) % length]]
    ppermute x2, waiting for transfers between devices: 3.08 us -> 1.12 us  [from_partner(): return lax.ppermute(block, axis, route)]
  transfers between devices with their start and end apart: 5 -> 11, of which waited for: 5 -> 8; matrix products, arithmetic and copies ran while one was open for 4% -> 10% of each run, Pallas kernels for 0% -> 0%
where the time goes in v1:
time: 114 us
  waiting for transfers between devices  68.2 us (60%)
  between operations  14.2 us (12%)
  starting transfers between devices  10.6 us (9%)
  local copies, waits for them, and re-layouts  9.88 us (9%)
  matrix products  7.86 us (7%)
  other arithmetic  3.16 us (3%)
    reduce_scatter x1, waiting for transfers between devices, local(): lax.psum_scatter(lax.dot_general(columns, flat_out, (((0,), (0,)), ((), (...  32.6 us
    ppermute x4, waiting for transfers between devices, gather_around(): lower.append(lax.ppermute(lower[-1] if lower else x, axis, pairs))  20 us
    all_gather x1, waiting for transfers between devices, local(): grad_full = lax.all_gather(grad_local, 'tensor', axis=0, tiled=True)  13.8 us
    ppermute x3, starting transfers between devices, gather_around(): upper.append(lax.ppermute(upper[-1] if upper else x, axis, back))  7.87 us
    unnamed x21, local copies, waits for them, and re-layouts  6.83 us
    dot_general x1, matrix products, local(): jnp.dot(columns, gather_around(out_weight, 'dp', 0), preferred_element_ty...  3.01 us
  transfers between devices with their start and end apart: 11, of which 8 were waited for; matrix products, arithmetic and copies ran while one was open for 10% of the time, Pallas kernels for 0%

profile of v1, /device:TPU:0, one launch (start us, length us, event | category | flops | bytes accessed | tf_op | source)
XLA Modules:
  0.0 113.9 jit_solution(6546431213387021698)
XLA Ops:
  7.2 0.7 all-gather.3.cloned.1.call-update
  8.0 0.5 collective-permute-start
  8.5 7.1 %collective-permute-done = bf16[512,256]{1,0:T(8,128)(2,1)S(1)} collective-permute-done((bf16[512,256]{1,0:T(8,128)(2,1)}, bf16[512,256]{1,0:T(8,128)(2,1)S(1)}, u32[]{:S(2)}, u32[]{:S(2)}) %collective-permute-start) | collective-permute-done | bytes 262176 | tf_op jit(solution)/shard_map/ppermute | solution.py:22
  15.6 2.6 %collective-permute-start.4 = (bf16[512,256]{1,0:T(8,128)(2,1)}, bf16[512,256]{1,0:T(8,128)(2,1)S(1)}, u32[]{:S(2)}, u32[]{:S(2)}) collective-permute-start(bf16[512,256]{1,0:T(8,128)(2,1)} %param.7), channel_id=1, source_target_pairs={{4,0},{8,4},{12,8},{16,12},{20,16},{24,20},{28,24},{0,28},{5,1},{9... | collective-permute-start | bytes 786440 | tf_op jit(solution)/shard_map/ppermute | solution.py:24
  18.3 4.9 %collective-permute-done.1 = bf16[512,256]{1,0:T(8,128)(2,1)S(1)} collective-permute-done((bf16[512,256]{1,0:T(8,128)(2,1)S(1)}, bf16[512,256]{1,0:T(8,128)(2,1)S(1)}, u32[]{:S(2)}, u32[]{:S(2)}) %collective-permute-start.1) | collective-permute-done | bytes 262176 | tf_op jit(solution)/shard_map/ppermute | solution.py:22
  23.2 0.9 fusion.16
  24.0 2.7 %collective-permute-start.5 = (bf16[512,256]{1,0:T(8,128)(2,1)S(1)}, bf16[512,256]{1,0:T(8,128)(2,1)}, u32[]{:S(2)}, u32[]{:S(2)}) collective-permute-start(bf16[512,256]{1,0:T(8,128)(2,1)S(1)} %collective-permute-done.4), channel_id=1, source_target_pairs={{4,0},{8,4},{12,8},{16,12},{20,16},{24,20},{28,24},{0,28},{5,1},{9... | collective-permute-start | bytes 786440 | tf_op jit(solution)/shard_map/ppermute | solution.py:24
  26.7 4.4 %collective-permute-done.2 = bf16[512,256]{1,0:T(8,128)(2,1)S(1)} collective-permute-done((bf16[512,256]{1,0:T(8,128)(2,1)S(1)}, bf16[512,256]{1,0:T(8,128)(2,1)S(1)}, u32[]{:S(2)}, u32[]{:S(2)}) %collective-permute-start.2) | collective-permute-done | bytes 262176 | tf_op jit(solution)/shard_map/ppermute | solution.py:22
  31.1 1.0 reshape_squeeze.3
  32.2 1.1 fusion.57
  33.3 2.5 %collective-permute-start.6 = (bf16[512,256]{1,0:T(8,128)(2,1)}, bf16[512,256]{1,0:T(8,128)(2,1)S(1)}, u32[]{:S(2)}, u32[]{:S(2)}) collective-permute-start(bf16[512,256]{1,0:T(8,128)(2,1)} %collective-permute-done.5), channel_id=1, source_target_pairs={{4,0},{8,4},{12,8},{16,12},{20,16},{24,20},{28,24},{0,28},{5,1},{9... | collective-permute-start | bytes 786440 | tf_op jit(solution)/shard_map/ppermute | solution.py:24
  35.8 3.6 %collective-permute-done.3 = bf16[512,256]{1,0:T(8,128)(2,1)} collective-permute-done((bf16[512,256]{1,0:T(8,128)(2,1)S(1)}, bf16[512,256]{1,0:T(8,128)(2,1)}, u32[]{:S(2)}, u32[]{:S(2)}) %collective-permute-start.3) | collective-permute-done | bytes 262176 | tf_op jit(solution)/shard_map/ppermute | solution.py:22
  39.4 1.0 bitcast_dynamic-update-slice_fusion.7
  40.4 1.0 bitcast_dynamic-update-slice_fusion.6
  41.5 1.0 bitcast_dynamic-update-slice_fusion.1
  42.5 2.0 %gather_fusion = bf16[8,512,256]{2,1,0:T(8,128)(2,1)} fusion(bf16[8,512,256]{2,1,0:T(8,128)(2,1)S(1)} %bitcast_dynamic-update-slice_fusion, s32[1024]{0:T(1024)S(1)} %pad_clamp_fusion), kind=kCustom, calls=%fused_computation | custom fusion | bytes 4194336 | tf_op jit(solution)/shard_map/gather | solution.py:27
  44.5 13.8 %all-gather.3.cloned.1.call-done = bf16[1,256,4096]{2,1,0:T(8,128)(2,1)} async-done(((bf16[1,64,4096]{2,1,0:T(8,128)(2,1)}), bf16[1,256,4096]{2,1,0:T(8,128)(2,1)}) %all-gather.3.cloned.1.call-update) | async-done | bytes 2097168 | tf_op jit(solution)/shard_map/all_gather | solution.py:67
  58.3 3.0 %fusion.13 = bf16[256,256]{1,0:T(8,128)(2,1)S(1)} fusion(bf16[4096,256]{1,0:T(8,128)(2,1)} %bitcast.123, bf16[1,256,4096]{2,1,0:T(8,128)(2,1)} %all-gather.3.cloned.1.call-done), kind=kOutput, calls=%fused_computation.19 | convolution fusion | flops 536936448 | bytes 4325376 | tf_op jit(solution)/shard_map/dot_general | solution.py:69
  61.3 0.5 multiply_reduce_fusion
  61.8 1.0 copy-done.1
  62.9 2.1 %fusion.1 = bf16[4096,256]{0,1:T(8,128)(2,1)} fusion(bf16[256,256]{0,1:T(8,128)(2,1)S(1)} %bitcast.125, bf16[1,256,4096]{2,1,0:T(8,128)(2,1)S(1)} %copy-done.1), kind=kOutput, calls=%fused_computation.3 | convolution fusion | flops 537919488 | bytes 4325376 | tf_op jit(solution)/shard_map/dot_general | solution.py:74
  65.0 1.0 copy-done.5
  66.5 0.2 convolution_convert_fusion.1
  66.7 0.5 fusion.67
  67.3 2.1 %collective-permute-start.8 = (bf16[256,128]{1,0:T(8,128)(2,1)S(1)}, bf16[256,128]{1,0:T(8,128)(2,1)S(1)}, u32[]{:S(2)}, u32[]{:S(2)}) collective-permute-start(bf16[256,128]{1,0:T(8,128)(2,1)S(1)} %get-tuple-element.14), channel_id=1, source_target_pairs={{0,1},{1,0},{2,3},{3,2},{4,5},{5,4},{6,7},{7,6},{8,9},{9,8},{10,11... | collective-permute-start | bytes 196616 | tf_op jit(solution)/shard_map/ppermute | solution.py:38
  69.3 0.8 copy.19
  70.1 1.1 collective-permute-done.7
  71.2 0.6 fusion.20
  71.9 0.6 fusion.21
  72.5 32.6 %reduce-scatter.2.cloned.1.call-done = bf16[512,256]{0,1:T(8,128)(2,1)} async-done(((bf16[4096,256]{0,1:T(8,128)(2,1)}), bf16[512,256]{0,1:T(8,128)(2,1)}) %reduce-scatter.2.cloned.1.call-update) | async-done | bytes 262160 | tf_op jit(solution)/shard_map/reduce_scatter | solution.py:73
  105.1 1.0 convert_multiply_fusion
  106.1 1.0 copy.20
  (30 shorter events, 0.8 us)
Async XLA Ops:
  7.2 25.0 %copy-start = (bf16[1,256,128]{2,1,0:T(8,128)(2,1)S(1)}, bf16[1,256,128]{2,1,0:T(8,128)(2,1)}, u32[]{:S(2)}) copy-start(bf16[1,256,128]{2,1,0:T(8,128)(2,1)} %param.9) | copy-start | bytes 196612
  7.2 34.3 %copy-start.2 = (bf16[512,256]{1,0:T(8,128)(2,1)S(1)}, bf16[512,256]{1,0:T(8,128)(2,1)}, u32[]{:S(2)}) copy-start(bf16[512,256]{1,0:T(8,128)(2,1)} %param.7) | copy-start | bytes 786436
  7.2 51.1 %all-gather.3.cloned.1.call-start = ((), (), s32[]{:S(2)}) async-start(), calls=%async_computation.2 | async-start | bytes 2621440 | tf_op jit(solution)/shard_map/all_gather | solution.py:67
  7.9 97.1 %reduce-scatter.2.cloned.1.call-start = ((), (), s32[]{:S(2)}) async-start(), calls=%async_computation.1 | async-start | bytes 2359296 | tf_op jit(solution)/shard_map/reduce_scatter | solution.py:73
  8.0 7.7 %collective-permute-start = (bf16[512,256]{1,0:T(8,128)(2,1)}, bf16[512,256]{1,0:T(8,128)(2,1)S(1)}, u32[]{:S(2)}, u32[]{:S(2)}) collective-permute-start(bf16[512,256]{1,0:T(8,128)(2,1)} %param.7), channel_id=1, source_target_pairs={{0,4},{4,8},{8,12},{12,16},{16,20},{20,24},{24,28},{28,0},{1,5},{5... | collective-permute-start | bytes 786440 | tf_op jit(solution)/shard_map/ppermute | solution.py:22
  15.6 7.5 %collective-permute-start.1 = (bf16[512,256]{1,0:T(8,128)(2,1)S(1)}, bf16[512,256]{1,0:T(8,128)(2,1)S(1)}, u32[]{:S(2)}, u32[]{:S(2)}) collective-permute-start(bf16[512,256]{1,0:T(8,128)(2,1)S(1)} %collective-permute-done), channel_id=1, source_target_pairs={{0,4},{4,8},{8,12},{12,16},{16,20},{20,24},{24,28},{28,0},{1,5},{5... | collective-permute-start | bytes 786440 | tf_op jit(solution)/shard_map/ppermute | solution.py:22
  15.6 8.4 %collective-permute-start.4 = (bf16[512,256]{1,0:T(8,128)(2,1)}, bf16[512,256]{1,0:T(8,128)(2,1)S(1)}, u32[]{:S(2)}, u32[]{:S(2)}) collective-permute-start(bf16[512,256]{1,0:T(8,128)(2,1)} %param.7), channel_id=1, source_target_pairs={{4,0},{8,4},{12,8},{16,12},{20,16},{24,20},{28,24},{0,28},{5,1},{9... | collective-permute-start | bytes 786440 | tf_op jit(solution)/shard_map/ppermute | solution.py:24
  23.2 8.0 %collective-permute-start.2 = (bf16[512,256]{1,0:T(8,128)(2,1)S(1)}, bf16[512,256]{1,0:T(8,128)(2,1)S(1)}, u32[]{:S(2)}, u32[]{:S(2)}) collective-permute-start(bf16[512,256]{1,0:T(8,128)(2,1)S(1)} %collective-permute-done.1), channel_id=1, source_target_pairs={{0,4},{4,8},{8,12},{12,16},{16,20},{20,24},{24,28},{28,0},{1,5},{5... | collective-permute-start | bytes 786440 | tf_op jit(solution)/shard_map/ppermute | solution.py:22
  24.0 9.2 %collective-permute-start.5 = (bf16[512,256]{1,0:T(8,128)(2,1)S(1)}, bf16[512,256]{1,0:T(8,128)(2,1)}, u32[]{:S(2)}, u32[]{:S(2)}) collective-permute-start(bf16[512,256]{1,0:T(8,128)(2,1)S(1)} %collective-permute-done.4), channel_id=1, source_target_pairs={{4,0},{8,4},{12,8},{16,12},{20,16},{24,20},{28,24},{0,28},{5,1},{9... | collective-permute-start | bytes 786440 | tf_op jit(solution)/shard_map/ppermute | solution.py:24
  31.1 4.7 %copy-start.3 = (bf16[512,256]{1,0:T(8,128)(2,1)}, bf16[512,256]{1,0:T(8,128)(2,1)S(1)}, u32[]{:S(2)}) copy-start(bf16[512,256]{1,0:T(8,128)(2,1)S(1)} %collective-permute-done.2) | copy-start | bytes 786436
  31.1 8.3 %collective-permute-start.3 = (bf16[512,256]{1,0:T(8,128)(2,1)S(1)}, bf16[512,256]{1,0:T(8,128)(2,1)}, u32[]{:S(2)}, u32[]{:S(2)}) collective-permute-start(bf16[512,256]{1,0:T(8,128)(2,1)S(1)} %collective-permute-done.2), channel_id=1, source_target_pairs={{0,4},{4,8},{8,12},{12,16},{16,20},{20,24},{24,28},{28,0},{1,5},{5... | collective-permute-start | bytes 786440 | tf_op jit(solution)/shard_map/ppermute | solution.py:22
  33.3 9.2 %collective-permute-start.6 = (bf16[512,256]{1,0:T(8,128)(2,1)}, bf16[512,256]{1,0:T(8,128)(2,1)S(1)}, u32[]{:S(2)}, u32[]{:S(2)}) collective-permute-start(bf16[512,256]{1,0:T(8,128)(2,1)} %collective-permute-done.5), channel_id=1, source_target_pairs={{4,0},{8,4},{12,8},{16,12},{20,16},{24,20},{28,24},{0,28},{5,1},{9... | collective-permute-start | bytes 786440 | tf_op jit(solution)/shard_map/ppermute | solution.py:24
  58.3 3.0 %copy-start.4 = (bf16[1,256,128]{2,1,0:T(8,128)(2,1)S(1)}, bf16[1,256,128]{2,1,0:T(8,128)(2,1)}, u32[]{:S(2)}) copy-start(bf16[1,256,128]{2,1,0:T(8,128)(2,1)} %param.10) | copy-start | bytes 196612
  61.3 1.6 %copy-start.1 = (bf16[1,256,4096]{2,1,0:T(8,128)(2,1)S(1)}, bf16[1,256,4096]{2,1,0:T(8,128)(2,1)}, u32[]{:S(2)}) copy-start(bf16[1,256,4096]{2,1,0:T(8,128)(2,1)} %all-gather.3.cloned.1.call-done) | copy-start | bytes 6291460
  64.9 1.0 copy-start.5
  66.4 4.7 %collective-permute-start.7 = (bf16[256,128]{1,0:T(8,128)(2,1)S(1)}, bf16[256,128]{1,0:T(8,128)(2,1)S(1)}, u32[]{:S(2)}, u32[]{:S(2)}) collective-permute-start(bf16[256,128]{1,0:T(8,128)(2,1)S(1)} %get-tuple-element.12), channel_id=1, source_target_pairs={{0,1},{1,0},{2,3},{3,2},{4,5},{5,4},{6,7},{7,6},{8,9},{9,8},{10,11... | collective-permute-start | bytes 196616 | tf_op jit(solution)/shard_map/ppermute | solution.py:38
  67.3 4.6 %collective-permute-start.8 = (bf16[256,128]{1,0:T(8,128)(2,1)S(1)}, bf16[256,128]{1,0:T(8,128)(2,1)S(1)}, u32[]{:S(2)}, u32[]{:S(2)}) collective-permute-start(bf16[256,128]{1,0:T(8,128)(2,1)S(1)} %get-tuple-element.14), channel_id=1, source_target_pairs={{0,1},{1,0},{2,3},{3,2},{4,5},{5,4},{6,7},{7,6},{8,9},{9,8},{10,11... | collective-permute-start | bytes 196616 | tf_op jit(solution)/shard_map/ppermute | solution.py:38
Sparse Core Ops, SparseCore 0:
  9.6 48.6 all-gather.2
  65.1 39.9 reduce-scatter.1
